TPU v7x, 256 devices: a whole 4x4x8 slice. The times are simulated.
256 devices in a mesh: rep: 16 (over y, x_hi, core), fsdp: 16 (over x_lo, z).
Axes of the slice: x: 4 (x_hi: 2, x_lo: 2; x = x_hi * 2 + x_lo), y: 4, z: 8, core: 2. Of those that a mesh axis runs over, the one named last changes fastest.
Arguments:
- inputs: bfloat16 [32768, 6656], P(('rep', 'fsdp')), may hold values from -40 to 40, as said below
- cotangent: bfloat16 [32768, 3328], P(('rep', 'fsdp')), may hold values from -6 to 6
- weight: bfloat16 [16, 6656, 3328], P('rep', 'fsdp'), may hold values from -6 to 6
- gain: bfloat16 [16, 6656], P('rep', 'fsdp'), may hold values from 0.25 to 1.75
- step: int32 [1], replicated, may hold values from 0 to 1048575
Outputs:
- input_gradient: bfloat16 [32768, 6656], P(('rep', 'fsdp'))
- weight_out: bfloat16 [16, 6656, 3328], P('rep', 'fsdp')
- gain_out: bfloat16 [16, 6656], P('rep', 'fsdp')
Inputs may be any that keep to these rules, and one draw needn't show every extreme that they name: `inputs`: entries of order one times a per-token and a per-feature scale that differ over a factor of ten.
All inputs are finite; a program needn't handle non-finite values.
Results may differ from a plain program's by a relative error of at most 0.0053.
Values may be sent and summed in bfloat16 or wider, within the bound.
A program may use at most 128 MiB of HBM per device.

v0:
```python
from functools import partial

import jax
import jax.numpy as jnp
from jax import lax
from jax.experimental import pallas as pl
from jax.experimental.pallas import tpu as pltpu
from jax.sharding import PartitionSpec as P

MESH = pl.DeviceIdType.MESH
F32 = jnp.float32
BF16 = jnp.bfloat16

epsilon = 1e-05
learn_rate = 0.5
gain_rate = 0.01

COLS = 2
RING = 8
CHUNKS = 4
PARTS = 2
PAIRS = RING // 2


def tiles(width, step):
    return [(at, min(step, width - at)) for at in range(0, width, step)]


def column_of(row):
    n = row.shape[1]
    i = lax.broadcasted_iota(jnp.int32, (n, n), 0)
    j = lax.broadcasted_iota(jnp.int32, (n, n), 1)
    return jnp.sum(jnp.where(i == j, row, 0.0), axis=1, keepdims=True)


def row_of(column):
    n = column.shape[0]
    i = lax.broadcasted_iota(jnp.int32, (n, n), 0)
    j = lax.broadcasted_iota(jnp.int32, (n, n), 1)
    return jnp.sum(jnp.where(i == j, column, 0.0), axis=0, keepdims=True)


def chunk_sizes(width):
    blocks = width // 128
    return [128 * (blocks // CHUNKS + (h < blocks % CHUNKS)) for h in range(CHUNKS)]


def body(
    offset,
    x_hbm, cot_hbm, w_hbm, gain_ref,
    ig_hbm, wout_hbm, gout_ref,
    cot, w, acc, pw, gp, nw, got,
    xin, xt, xc, xn, fg, gg, gb, dxt, ret, gbuf, gsum, ng,
    local_sem, ag_send, ag_recv, w_send, w_recv, x_send, x_recv, p_send, p_recv,
    r_send, r_recv, g_send, g_recv, s_send, s_recv,
):
    rows, width = xin.shape
    feat = xc.shape[2]
    sizes = [c.shape[2] for c in cot]
    starts = [sum(sizes[:h]) for h in range(CHUNKS)]
    factor = width ** (-0.5)
    part_rows = feat // PARTS

    reps = lax.axis_size("rep")
    rep = lax.axis_index("rep")
    me = lax.axis_index("fsdp")
    col = me // RING
    z = me % RING
    across = (rep, (1 - col) * RING + z)
    to_rep = (rep + offset) % reps
    from_rep = (rep + reps - offset) % reps

    def remote(src, dst, send_sem, recv_sem, device):
        return pltpu.make_async_remote_copy(
            src_ref=src, dst_ref=dst, send_sem=send_sem, recv_sem=recv_sem,
            device_id=device, device_id_type=MESH,
        )

    barrier = pltpu.get_barrier_semaphore()
    for k in range(1, RING):
        pl.semaphore_signal(
            barrier, inc=1, device_id=(rep, col * RING + (z + k) % RING), device_id_type=MESH
        )
    for device in (across, (to_rep, me), (from_rep, me)):
        pl.semaphore_signal(barrier, inc=1, device_id=device, device_id_type=MESH)

    in_cot = [
        pltpu.make_async_copy(cot_hbm.at[:, pl.ds(starts[h], sizes[h])], cot[h].at[z], local_sem.at[h])
        for h in range(CHUNKS)
    ]
    in_w = [
        pltpu.make_async_copy(
            w_hbm.at[:, pl.ds(starts[h], sizes[h])], w[h].at[col], local_sem.at[CHUNKS + h]
        )
        for h in range(CHUNKS)
    ]
    in_x = pltpu.make_async_copy(x_hbm, xin, local_sem.at[2 * CHUNKS])
    in_cot[0].start()
    in_x.start()
    for h in range(CHUNKS):
        in_w[h].start()
    for h in range(1, CHUNKS):
        in_cot[h].start()
    gbuf[col] = jnp.zeros(gbuf.shape[1:], F32)
    gbuf[col, 0:1, 0:feat] = gain_ref[...].astype(F32)

    pl.semaphore_wait(barrier, RING + 2)

    def sign(p):
        return 1 - 2 * p

    def origin(p, d):
        return (z + 2 * RING - sign(p) * d) % RING

    def half_block(h, d, p):
        return cot[h].at[origin(p, d), pl.ds(p * (rows // 2), rows // 2), :]

    def recv_of(h, d, p):
        return ag_recv.at[(h * 2 + p) * RING + origin(p, d)]

    def ag_copy(h, d, p, way, number):
        step = sign(p) if way == "lead" else -sign(p)
        return remote(
            half_block(h, d, p), half_block(h, d, p), ag_send.at[number], recv_of(h, d, p),
            (rep, col * RING + (z + RING + step) % RING),
        )

    sent = []

    def send(h, d, p, way):
        sent.append((h, d, p, way))
        ag_copy(h, d, p, way, len(sent) - 1).start()

    def arrived(h, d, p):
        remote(
            half_block(h, d, p), half_block(h, d, p), ag_send.at[0], recv_of(h, d, p), across
        ).wait_recv()

    def ring_start(h):
        in_cot[h].wait()
        for way in ("lead", "trail"):
            for p in range(2):
                send(h, 0, p, way)

    def ring_step(h, k):
        for p in range(2):
            arrived(h, k, p)
            if k <= 3:
                send(h, k, p, "lead")
        if k <= 3:
            for p in range(2):
                arrived(h, -k, p)
                if k <= 2:
                    send(h, -k, p, "trail")

    ring_start(0)

    in_x.wait()
    lanes = 512 if width % 512 == 0 else 128

    def square(k, total):
        part = xin[:, pl.ds(pl.multiple_of(k * lanes, lanes), lanes)].astype(F32)
        part = part * part
        for at, size in tiles(lanes, 128):
            total = total + part[:, at : at + size]
        return total

    total = lax.fori_loop(0, width // lanes, square, jnp.zeros((rows, 128), F32))
    rstd = lax.rsqrt(jnp.sum(total, axis=1, keepdims=True) / width + epsilon)
    side = width // COLS // 128

    def normalize(k, carry):
        for c in range(COLS):
            at = pl.multiple_of((c * side + k) * 128, 128)
            part = (xin[:, pl.ds(at, 128)].astype(F32) * rstd).astype(BF16).astype(F32)
            xt[c, pl.ds(pl.multiple_of(k * 128, 128), 128), :] = part.T.astype(BF16)
        return carry

    lax.fori_loop(0, side, normalize, 0)

    def feat_rows(j):
        return pl.ds(pl.multiple_of(j * feat, 16), feat)

    def x_copy(k):
        j = (z + k) % RING
        return remote(
            xt.at[:, feat_rows(j), :], xc.at[z], x_send.at[k], x_recv.at[z], (rep, col * RING + j)
        )

    def x_arrived(j):
        remote(xc.at[j], xc.at[j], x_send.at[0], x_recv.at[j], across).wait_recv()

    def start_x(k, carry):
        x_copy(k).start()
        return carry

    lax.fori_loop(1, RING, start_x, 0)
    own_x = pltpu.make_async_copy(xt.at[:, feat_rows(z), :], xc.at[z], local_sem.at[2 * CHUNKS])
    own_x.start()

    gain_copy = remote(gbuf.at[col], gbuf.at[col], s_send.at[0], s_recv.at[0], across)
    gain_copy.start()

    def w_copy(h):
        return remote(w[h].at[col], w[h].at[col], w_send.at[h], w_recv.at[h], across)

    for h in range(CHUNKS):
        in_w[h].wait()
        w_copy(h).start()

    gg[...] = jnp.zeros_like(gg)
    own_x.wait()

    def rows_of(p):
        return pl.ds(p * part_rows, part_rows)

    def p_copy(h, p):
        number = h * PARTS + p
        return remote(
            pw[h].at[rows_of(p), :], gp[h].at[rows_of(p), :], p_send.at[number], p_recv.at[number], across
        )

    def g_copy(h, p):
        number = h * PARTS + p
        return remote(
            nw[h].at[rows_of(p), :], got[h].at[rows_of(p), :], g_send.at[number], g_recv.at[number],
            (to_rep, me),
        )

    def by_rows(p, work):
        def some(k, carry):
            work(pl.ds(pl.multiple_of(p * part_rows + k * 16, 16), 16))
            return carry

        lax.fori_loop(0, part_rows // 16, some, 0)

    def hand_over(h):
        for p in range(PARTS):

            def work(at):
                pw[h][at, :] = acc[h][1 - col, at, :].astype(BF16)

            by_rows(p, work)
            p_copy(h, p).start()

    def update(h):
        for p in range(PARTS):
            p_copy(h, p).wait_recv()

            def work(at):
                whole = acc[h][col, at, :] + gp[h][at, :].astype(F32)
                old = w[h][col, at, :].astype(F32)
                nw[h][at, :] = (old - learn_rate * (factor * whole)).astype(BF16)

            by_rows(p, work)
            g_copy(h, p).start()

    out_w = []

    def average(h):
        for p in range(PARTS):
            g_copy(h, p).wait_recv()

            def work(at):
                both = nw[h][at, :].astype(F32) + got[h][at, :].astype(F32)
                gp[h][at, :] = (both * 0.5).astype(BF16)

            by_rows(p, work)
            copy = pltpu.make_async_copy(
                gp[h].at[rows_of(p), :],
                wout_hbm.at[rows_of(p), pl.ds(starts[h], sizes[h])],
                local_sem.at[2 * CHUNKS + 1 + h * PARTS + p],
            )
            copy.start()
            out_w.append(copy)

    def r_copy(j):
        return remote(
            dxt.at[j], ret.at[:, feat_rows(z), :], r_send.at[j], r_recv.at[z], (rep, col * RING + j)
        )

    own_r = pltpu.make_async_copy(dxt.at[z], ret.at[:, feat_rows(z), :], local_sem.at[2 * CHUNKS])

    def pair_of(t):
        return (z + RING - (t + 1)) % RING, (z + (t + 1) % PAIRS) % RING

    def weight_step(h, events, t, carry):
        for at, event in events:
            pl.when(t == at)(event)
        a, b = pair_of(t)
        if h == 0:
            x_arrived(a)

            @pl.when(t < PAIRS - 1)
            def _():
                x_arrived(b)

        @pl.when(t == 0)
        def _():
            def clear(k, carry):
                acc[h][:, pl.ds(pl.multiple_of(k * 16, 16), 16), :] = jnp.zeros((COLS, 16, sizes[h]), F32)
                return carry

            lax.fori_loop(0, feat // 16, clear, 0)

        def side_sum(c, carry):
            if h == 0:
                for j in (a, b):
                    xn[j, c] = (xc[j, c].astype(F32) * gb[c]).astype(BF16)
            lhs = jnp.concatenate([xn[a, c], xn[b, c]], axis=1)
            for at, n in tiles(sizes[h], 256):
                ct = jnp.concatenate([cot[h][a, :, pl.ds(at, n)], cot[h][b, :, pl.ds(at, n)]], axis=0)
                acc[h][c, :, pl.ds(at, n)] += jnp.dot(lhs, ct, preferred_element_type=F32)
            return carry

        return lax.fori_loop(0, COLS, side_sum, carry)

    def feature_step(h, t, carry):
        a, b = pair_of(t)
        ct = jnp.concatenate([cot[h][a], cot[h][b]], axis=0)
        def side_feature(c, carry):
            feature = lax.dot_general(
                w[h][c], ct, (((1,), (1,)), ((), ())), preferred_element_type=F32
            )
            if h == 0:
                fg[a, c] = feature[:, :rows]
                fg[b, c] = feature[:, rows:]
            elif h < CHUNKS - 1:
                fg[a, c] += feature[:, :rows]
                fg[b, c] += feature[:, rows:]
            else:
                for j, part in ((a, feature[:, :rows]), (b, feature[:, rows:])):
                    whole = factor * (fg[j, c] + part)
                    gg[c] += whole * xc[j, c].astype(F32)
                    dxt[j, c] = (whole * gb[c]).astype(BF16)
            return carry

        lax.fori_loop(0, COLS, side_feature, 0)
        if h == CHUNKS - 1:
            r_copy(a).start()

            @pl.when(t < PAIRS - 1)
            def _():
                r_copy(b).start()

        return carry

    def weight_sums(h, *events):
        lax.fori_loop(0, PAIRS, partial(weight_step, h, events), 0)

    def features(h):
        w_copy(h).wait_recv()
        lax.fori_loop(0, PAIRS, partial(feature_step, h), 0)

    ring_step(0, 1)
    ring_step(0, 2)
    ring_step(0, 3)
    ring_start(1)
    ring_step(0, 4)
    gain_copy.wait_recv()

    def spread(c, carry):
        gb[c] = jnp.broadcast_to(column_of(gbuf[c, 0:1, 0:feat]), gb.shape[1:])
        return carry

    lax.fori_loop(0, COLS, spread, 0)

    def turn_2():
        ring_start(2)
        ring_step(1, 2)

    weight_sums(0, (1, lambda: ring_step(1, 1)), (3, turn_2))
    hand_over(0)
    ring_step(1, 3)
    ring_start(3)
    ring_step(2, 1)
    ring_step(1, 4)
    weight_sums(1, (2, lambda: ring_step(2, 2)))
    hand_over(1)
    ring_step(3, 1)
    update(0)
    ring_step(2, 3)
    features(0)
    ring_step(3, 2)
    ring_step(2, 4)
    weight_sums(2)
    hand_over(2)
    ring_step(3, 3)
    update(1)
    features(1)
    features(2)
    w_copy(3).wait_recv()

    def last_step(t, carry):
        weight_step(3, (), t, 0)
        feature_step(3, t, 0)
        return carry

    lax.fori_loop(0, PAIRS - 1, last_step, 0)
    ring_step(3, 4)
    feature_step(3, jnp.int32(PAIRS - 1), 0)
    own_r.start()
    weight_step(3, (), jnp.int32(PAIRS - 1), 0)
    hand_over(3)
    update(2)

    def gain_sum(k, carry):
        side_of = (1 - col) * (1 - k) + col * k
        gsum[2 * k] = jnp.zeros(gsum.shape[1:], F32)
        gsum[2 * k, 0:1, 0:feat] = row_of(jnp.sum(gg[side_of], axis=1, keepdims=True))
        return carry

    lax.fori_loop(0, 2, gain_sum, 0)
    sum_copy = remote(gsum.at[0], gsum.at[1], s_send.at[1], s_recv.at[1], across)
    sum_copy.start()
    sum_copy.wait_recv()
    total_gain = gsum[2, 0:1, 0:feat] + gsum[1, 0:1, 0:feat]
    new_gain = (gbuf[col, 0:1, 0:feat] - gain_rate * total_gain).astype(BF16).astype(F32)
    ng[0] = jnp.zeros(ng.shape[1:], F32)
    ng[0, 0:1, 0:feat] = new_gain
    new_gain_copy = remote(ng.at[0], ng.at[1], s_send.at[2], s_recv.at[2], (to_rep, me))
    new_gain_copy.start()
    average(0)
    update(3)
    average(1)
    average(2)

    for number, (h, d, p, way) in enumerate(sent):
        ag_copy(h, d, p, way, number).wait_send()
    for h in range(CHUNKS):
        w_copy(h).wait_send()
    gain_copy.wait_send()

    def drain_x(k, carry):
        x_copy(k).wait_send()
        return carry

    lax.fori_loop(1, RING, drain_x, 0)

    def add_part(j, inner):
        for c in range(COLS):
            prod = ret[c, feat_rows(j), :].astype(F32) * xt[c, feat_rows(j), :].astype(F32)
            inner = inner + jnp.sum(prod.reshape(feat // 8, 8, rows), axis=0)
        return inner

    own_r.wait()
    inner = add_part(z, jnp.zeros((8, rows), F32))

    def add_return(k, inner):
        j = (z + k) % RING
        remote(dxt.at[0], ret.at[:, feat_rows(j), :], r_send.at[0], r_recv.at[j], across).wait_recv()
        return add_part(j, inner)

    average(3)
    inner = lax.fori_loop(1, RING, add_return, inner)
    mean = jnp.sum(inner, axis=0, keepdims=True) / width

    out_x = []
    for c in range(COLS):

        def finish(k, carry):
            at = pl.ds(pl.multiple_of(k * 128, 128), 128)
            part = ret[c, at, :].astype(F32) - xt[c, at, :].astype(F32) * mean
            xin[:, pl.ds(pl.multiple_of((c * side + k) * 128, 128), 128)] = (part.T * rstd).astype(BF16)
            return carry

        lax.fori_loop(0, side, finish, 0, unroll=2)
        half = pl.ds(c * side * 128, side * 128)
        copy = pltpu.make_async_copy(xin.at[:, half], ig_hbm.at[:, half], local_sem.at[2 * CHUNKS - 1 - c])
        copy.start()
        out_x.append(copy)
    new_gain_copy.wait_recv()
    gout_ref[...] = (new_gain + ng[1, 0:1, 0:feat]) * 0.5

    for h in range(CHUNKS):
        for p in range(PARTS):
            p_copy(h, p).wait_send()
            g_copy(h, p).wait_send()
    for copy in (sum_copy, new_gain_copy):
        copy.wait_send()

    def drain_r(k, carry):
        r_copy((z + k) % RING).wait_send()
        return carry

    lax.fori_loop(1, RING, drain_r, 0)
    for copy in out_x + out_w:
        copy.wait()


def run(offset, call_id, inputs, cotangent, weight, gain):
    rows, width = inputs.shape
    feat, proj = weight.shape
    sizes = chunk_sizes(proj)
    any_space = pl.BlockSpec(memory_space=pl.ANY)
    vmem = pl.BlockSpec(memory_space=pltpu.VMEM)
    dma = pltpu.SemaphoreType.DMA

    def chunks(shape, dtype):
        return [pltpu.VMEM((*shape, n), dtype) for n in sizes]

    side = (COLS, width // COLS, rows)
    return pl.pallas_call(
        partial(body, offset),
        out_shape=(
            jax.ShapeDtypeStruct((rows, width), BF16),
            jax.ShapeDtypeStruct((feat, proj), BF16),
            jax.ShapeDtypeStruct((1, feat), F32),
        ),
        in_specs=[any_space, any_space, any_space, vmem],
        out_specs=(any_space, any_space, vmem),
        scratch_shapes=[
            chunks((RING, rows), BF16),
            chunks((COLS, feat), BF16),
            chunks((COLS, feat), F32),
            chunks((feat,), BF16),
            chunks((feat,), BF16),
            chunks((feat,), BF16),
            chunks((feat,), BF16),
            pltpu.VMEM((rows, width), BF16),
            pltpu.VMEM(side, BF16),
            pltpu.VMEM((RING, COLS, feat, rows), BF16),
            pltpu.VMEM((RING, COLS, feat, rows), BF16),
            pltpu.VMEM((RING, COLS, feat, rows), F32),
            pltpu.VMEM((COLS, feat, rows), F32),
            pltpu.VMEM((COLS, feat, 128), F32),
            pltpu.VMEM((RING, COLS, feat, rows), BF16),
            pltpu.VMEM(side, BF16),
            pltpu.VMEM((COLS, 8, 512), F32),
            pltpu.VMEM((3, 8, 512), F32),
            pltpu.VMEM((2, 8, 512), F32),
            dma((2 * CHUNKS + 1 + CHUNKS * PARTS,)),
            dma((14 * CHUNKS,)),
            dma((2 * RING * CHUNKS,)),
            dma((CHUNKS,)),
            dma((CHUNKS,)),
            dma((RING,)),
            dma((RING,)),
            dma((CHUNKS * PARTS,)),
            dma((CHUNKS * PARTS,)),
            dma((RING,)),
            dma((RING,)),
            dma((CHUNKS * PARTS,)),
            dma((CHUNKS * PARTS,)),
            dma((3,)),
            dma((3,)),
        ],
        compiler_params=pltpu.CompilerParams(
            collective_id=call_id, has_side_effects=True, vmem_limit_bytes=58 * 1024 * 1024
        ),
    )(inputs, cotangent, weight, gain)


def per_device(inputs, cotangent, weight, gain, step):
    levels = lax.axis_size("rep").bit_length() - 1
    exponent = jnp.remainder(step[0], levels)
    branches = [partial(run, 1 << level, 1 + level) for level in range(levels)]
    input_gradient, weight_out, gain_out = lax.switch(
        exponent, branches, inputs, cotangent, weight[0], gain
    )
    return (input_gradient, weight_out[None], gain_out.astype(BF16))


def solution(mesh):
    in_specs = (
        P(("rep", "fsdp"), None),
        P(("rep", "fsdp"), None),
        P("rep", "fsdp", None),
        P("rep", "fsdp"),
        P(),
    )
    out_specs = (P(("rep", "fsdp"), None), P("rep", "fsdp", None), P("rep", "fsdp"))
    return jax.shard_map(
        per_device, mesh=mesh, in_specs=in_specs, out_specs=out_specs, check_vma=False
    )
```

profile of v0, /device:TPU:2, one launch (start us, length us, event | category | flops | bytes accessed | tf_op | source)
XLA Modules:
  0.0 167.7 jit_solution(10678554392684790853)
XLA Ops:
  1.3 163.1 %conditional.2 = (bf16[128,6656]{1,0:T(8,128)(2,1)S(1)}, bf16[1,416,3328]{2,1,0:T(8,128)(2,1)S(1)}, f32[1,416]{1,0:T(1,128)S(1)}) conditional(s32[]{:T(128)} %clamp.3, (bf16[128,6656]{1,0:T(8,128)(2,1)}, bf16[128,3328]{1,0:T(8,128)(2,1)}, bf16[416,3328]{1,0:T(8,128)(2,1)}, bf16[1,416]{1,0:T(2,128)(2,1)}) %tuple.45, ...), branch_computations={%region_0.1_spmd, %region_1.2_spmd, %region_2.3_spmd, %region_3.4_... | conditional | bytes 24
  1.5 162.7 %branch_3_fun.1 = (bf16[128,6656]{1,0:T(8,128)(2,1)S(1)}, bf16[416,3328]{1,0:T(8,128)(2,1)S(1)}, f32[1,416]{1,0:T(1,128)S(1)}) custom-call(bf16[128,6656]{1,0:T(8,128)(2,1)} %get-tuple-element.71.x_hbm, bf16[128,3328]{1,0:T(8,128)(2,1)} %get-tuple-element.72.cot_hbm, bf16[416,3328]{1,0:T(8,128)(2,1)} %get-tuple-element.73.w_hbm, ...), custom_call_target="tpu_custom_call" | custom-call | tf_op jit(solution)/shard_map/cond/branch_3_fun/pallas_call | solution.py:503
  164.4 0.6 convert_element_type.8
  165.0 1.2 copy.23
  166.2 1.5 copy.24
where the time goes:
time: 168 us
  Pallas kernels  163 us (97%)
  local copies, waits for them, and re-layouts  2.72 us (2%)
    pallas_call x1, Pallas kernels, run(): pl.pallas_call(partial(body, offset), out_shape=(jax.ShapeDtypeStruct((ro...  163 us

commit v1 on v0

--- a/solution.py
+++ b/solution.py
@@ -42,7 +42,8 @@
 
 def chunk_sizes(width):
     blocks = width // 128
-    return [128 * (blocks // CHUNKS + (h < blocks % CHUNKS)) for h in range(CHUNKS)]
+    order = (1, 2, 0, 3)
+    return [128 * (blocks // CHUNKS + (order.index(h) < blocks % CHUNKS)) for h in range(CHUNKS)]
 
 
 def body(

time: 168 us -> 167 us (level)
  Pallas kernels: 163 us -> 161 us
where the time goes in v1:
time: 167 us
  Pallas kernels  161 us (96%)
  local copies, waits for them, and re-layouts  2.72 us (2%)
    pallas_call x1, Pallas kernels, run(): pl.pallas_call(partial(body, offset), out_shape=(jax.ShapeDtypeStruct((ro...  161 us

profile of v1, /device:TPU:2, one launch (start us, length us, event | category | flops | bytes accessed | tf_op | source)
XLA Modules:
  0.0 166.5 jit_solution(8381026430721143035)
XLA Ops:
  1.3 161.9 %conditional.2 = (bf16[128,6656]{1,0:T(8,128)(2,1)S(1)}, bf16[1,416,3328]{2,1,0:T(8,128)(2,1)S(1)}, f32[1,416]{1,0:T(1,128)S(1)}) conditional(s32[]{:T(128)} %clamp.3, (bf16[128,6656]{1,0:T(8,128)(2,1)}, bf16[128,3328]{1,0:T(8,128)(2,1)}, bf16[416,3328]{1,0:T(8,128)(2,1)}, bf16[1,416]{1,0:T(2,128)(2,1)}) %tuple.45, ...), branch_computations={%region_0.1_spmd, %region_1.2_spmd, %region_2.3_spmd, %region_3.4_... | conditional | bytes 24
  1.5 161.5 %branch_3_fun.1 = (bf16[128,6656]{1,0:T(8,128)(2,1)S(1)}, bf16[416,3328]{1,0:T(8,128)(2,1)S(1)}, f32[1,416]{1,0:T(1,128)S(1)}) custom-call(bf16[128,6656]{1,0:T(8,128)(2,1)} %get-tuple-element.71.x_hbm, bf16[128,3328]{1,0:T(8,128)(2,1)} %get-tuple-element.72.cot_hbm, bf16[416,3328]{1,0:T(8,128)(2,1)} %get-tuple-element.73.w_hbm, ...), custom_call_target="tpu_custom_call" | custom-call | tf_op jit(solution)/shard_map/cond/branch_3_fun/pallas_call | solution.py:504
  163.2 0.6 convert_element_type.8
  163.8 1.2 copy.23
  165.0 1.5 copy.24
